TPU v7x, 1024 devices: a whole 8x8x8 slice. The times are simulated.
1024 devices in a mesh: gx: 32 (over x, z_lo), gy: 32 (over z_hi, y, core).
Axes of the slice: x: 8, y: 8, z: 8 (z_hi: 2, z_lo: 4; z = z_hi * 4 + z_lo), core: 2. Of those that a mesh axis runs over, the one named last changes fastest.
Arguments:
- composition: float32 [53, 1024, 4096], P(None, 'gx', 'gy'), may hold values from -6 to 6
- inverse_temp: float32 [1024, 4096], P('gx', 'gy'), may hold values from 0.3 to 1.2
- sections: int32 [1024, 32], P('gx', 'gy'), may hold values from 2 to 12, as said below
- reactant_orders: float32 [325, 53], replicated, may hold values from -0.875 to 0.875
- net_stoich: float32 [53, 325], replicated, may hold values from -0.3125 to 0.3125
- log_prefactor: float32 [325], replicated, may hold values from -1 to 1
- activation: float32 [325], replicated, may hold values from 0.5 to 3
- diffusivity: float32 [53], replicated, may hold values from 0.04 to 0.2
Outputs:
- state_next: float32 [53, 1024, 4096], P(None, 'gx', 'gy')
Inputs may be any that keep to these rules, and one draw needn't show every extreme that they name: Every draw has blocks with 12 sections and blocks with 2 sections.
All inputs are finite; a program needn't handle non-finite values.
Results may differ from a plain program's by a relative error of at most 0.0003.
Values sent between devices are 32-bit elements; how exact they have to be, the bound alone decides.
A program may use at most 32 MiB of HBM per device.

v0:
```python
import jax
import jax.numpy as jnp
from jax import lax
from jax.sharding import PartitionSpec as P

spectrum_mid = 4.5
spectrum_half = 3.5


def padded_2(value, sides, width):
    for axis, dim in sides:
        count, length = (lax.axis_size(axis), value.shape[dim])
        up = [(i, (i + 1) % count) for i in range(count - 1)]
        down = [(j, i) for i, j in up]
        last = lax.slice_in_dim(value, length - width, length, axis=dim)
        leading = lax.slice_in_dim(value, 0, width, axis=dim)
        before = lax.ppermute(last, axis, up)
        after = lax.ppermute(leading, axis, down)
        value = jnp.concatenate([before, value, after], axis=dim)
    return value


def relax_group(
    start_state, theta_cells, counts_group, reactant_orders, net_stoich, log_prefactor, activation
):
    rate_cells = jnp.exp(log_prefactor[:, None] - activation[:, None] * theta_cells[None, :])
    cells_each = theta_cells.shape[0] // counts_group.shape[0]
    count_float = counts_group.astype(jnp.float32)

    def section(section_idx, current):
        cheb_node = jnp.cos(
            jnp.pi * (2 * section_idx + 1).astype(jnp.float32) / (2.0 * count_float)
        )
        step_size = 1.0 / (spectrum_mid + spectrum_half * cheb_node)
        step_size = jnp.where(section_idx < counts_group, step_size, 0.0)
        step_cells = jnp.repeat(step_size, cells_each)
        drive = jnp.dot(reactant_orders, current, precision=lax.Precision.HIGHEST)
        forward = rate_cells * jax.nn.sigmoid(drive)
        source = jnp.dot(net_stoich, forward, precision=lax.Precision.HIGHEST)
        return current - step_cells[None, :] * (current - start_state - source)

    return lax.fori_loop(0, jnp.max(counts_group), section, start_state)


def chem_blocks(
    block_state, block_temps, counts, reactant_orders, net_stoich, log_prefactor, activation, group
):
    species, block_count, cells = block_state.shape
    group_count = block_count // group
    block_order = jnp.argsort(-counts, stable=True)
    group_state = jnp.moveaxis(
        block_state[:, block_order].reshape(species, group_count, group * cells), 1, 0
    )
    group_temps = block_temps[block_order].reshape(group_count, group * cells)
    group_counts = counts[block_order].reshape(group_count, group)

    def run_group(group_item):
        return relax_group(
            group_item[0],
            group_item[1],
            group_item[2],
            reactant_orders,
            net_stoich,
            log_prefactor,
            activation,
        )

    relaxed = lax.map(run_group, (group_state, group_temps, group_counts))
    relaxed = jnp.moveaxis(relaxed, 0, 1).reshape(species, block_count, cells)
    inverse_order = jnp.argsort(block_order)
    return relaxed[:, inverse_order]


def body(
    composition,
    inverse_temp,
    sections,
    reactant_orders,
    net_stoich,
    log_prefactor,
    activation,
    diffusivity,
):
    counts = sections[:, 0]
    reacted = chem_blocks(
        composition, inverse_temp, counts, reactant_orders, net_stoich, log_prefactor, activation, 4
    )
    padded = padded_2(reacted, (("gx", 1), ("gy", 2)), 1)
    laplace_term = (
        padded[:, 2:, 1:-1]
        + padded[:, :-2, 1:-1]
        + padded[:, 1:-1, 2:]
        + padded[:, 1:-1, :-2]
        - 4.0 * reacted
    )
    return reacted + diffusivity[:, None, None] * laplace_term


def solution(mesh):
    return jax.shard_map(
        body,
        mesh=mesh,
        in_specs=(P(None, "gx", "gy"), P("gx", "gy"), P("gx", "gy"), P(), P(), P(), P(), P()),
        out_specs=P(None, "gx", "gy"),
        check_vma=False,
    )
```

profile of v0, /device:TPU:110, one launch (start us, length us, event | category | flops | bytes accessed | tf_op | source)
XLA Modules:
  0.0 273.0 jit_solution(17638550367109696879)
XLA Ops:
  0.7 1.6 sort.34
  2.4 1.6 sort.35
  5.4 2.4 gather_fusion
  8.8 181.9 %while.22 = (s32[]{:T(128)}, f32[8,53,512]{2,1,0:T(8,128)}, f32[8,53,512]{2,0,1:T(8,128)S(1)}, s32[8,4]{1,0:T(8,128)S(1)}, f32[325]{0:T(512)S(1)}, /*index=5*/f3...) while((s32[]{:T(128)}, f32[8,53,512]{2,1,0:T(8,128)}, ...), condition=%wide.region_5.6_spmd, body=%wide.region_1.5_spmd.sunk | while | flops 212767776 | bytes 2791130 | solution.py:68
  9.6 27.8 %while.23 = (s32[]{:T(128)}, f32[53,512]{1,0:T(8,128)S(1)}, s32[]{:T(128)}, s32[4]{0:T(128)S(1)}, f32[4]{0:T(128)S(1)}, /*index=5*/f32[53,512]{1,0:T(8,128)S(1)}...) while((s32[]{:T(128)}, f32[53,512]{1,0:T(8,128)S(1)}, ...), condition=%wide.region_4.4_spmd.clone, body=%wide.region_3.3_spmd.clone.sunk | while | flops 212767776 | bytes 1912177 | solution.py:42
  10.4 0.9 fusion.37
  12.6 0.9 fusion.37
  14.9 0.9 fusion.37
  17.2 0.9 fusion.37
  38.9 25.5 %while.23 = (s32[]{:T(128)}, f32[53,512]{1,0:T(8,128)S(1)}, s32[]{:T(128)}, s32[4]{0:T(128)S(1)}, f32[4]{0:T(128)S(1)}, /*index=5*/f32[53,512]{1,0:T(8,128)S(1)}...) while((s32[]{:T(128)}, f32[53,512]{1,0:T(8,128)S(1)}, ...), condition=%wide.region_4.4_spmd.clone, body=%wide.region_3.3_spmd.clone.sunk | while | flops 212767776 | bytes 1912177 | solution.py:42
  39.6 0.9 fusion.37
  65.9 23.3 %while.23 = (s32[]{:T(128)}, f32[53,512]{1,0:T(8,128)S(1)}, s32[]{:T(128)}, s32[4]{0:T(128)S(1)}, f32[4]{0:T(128)S(1)}, /*index=5*/f32[53,512]{1,0:T(8,128)S(1)}...) while((s32[]{:T(128)}, f32[53,512]{1,0:T(8,128)S(1)}, ...), condition=%wide.region_4.4_spmd.clone, body=%wide.region_3.3_spmd.clone.sunk | while | flops 212767776 | bytes 1912177 | solution.py:42
  90.6 21.0 %while.23 = (s32[]{:T(128)}, f32[53,512]{1,0:T(8,128)S(1)}, s32[]{:T(128)}, s32[4]{0:T(128)S(1)}, f32[4]{0:T(128)S(1)}, /*index=5*/f32[53,512]{1,0:T(8,128)S(1)}...) while((s32[]{:T(128)}, f32[53,512]{1,0:T(8,128)S(1)}, ...), condition=%wide.region_4.4_spmd.clone, body=%wide.region_3.3_spmd.clone.sunk | while | flops 212767776 | bytes 1912177 | solution.py:42
  113.0 21.0 %while.23 = (s32[]{:T(128)}, f32[53,512]{1,0:T(8,128)S(1)}, s32[]{:T(128)}, s32[4]{0:T(128)S(1)}, f32[4]{0:T(128)S(1)}, /*index=5*/f32[53,512]{1,0:T(8,128)S(1)}...) while((s32[]{:T(128)}, f32[53,512]{1,0:T(8,128)S(1)}, ...), condition=%wide.region_4.4_spmd.clone, body=%wide.region_3.3_spmd.clone.sunk | while | flops 212767776 | bytes 1912177 | solution.py:42
  135.5 18.7 %while.23 = (s32[]{:T(128)}, f32[53,512]{1,0:T(8,128)S(1)}, s32[]{:T(128)}, s32[4]{0:T(128)S(1)}, f32[4]{0:T(128)S(1)}, /*index=5*/f32[53,512]{1,0:T(8,128)S(1)}...) while((s32[]{:T(128)}, f32[53,512]{1,0:T(8,128)S(1)}, ...), condition=%wide.region_4.4_spmd.clone, body=%wide.region_3.3_spmd.clone.sunk | while | flops 212767776 | bytes 1912177 | solution.py:42
  155.7 16.5 %while.23 = (s32[]{:T(128)}, f32[53,512]{1,0:T(8,128)S(1)}, s32[]{:T(128)}, s32[4]{0:T(128)S(1)}, f32[4]{0:T(128)S(1)}, /*index=5*/f32[53,512]{1,0:T(8,128)S(1)}...) while((s32[]{:T(128)}, f32[53,512]{1,0:T(8,128)S(1)}, ...), condition=%wide.region_4.4_spmd.clone, body=%wide.region_3.3_spmd.clone.sunk | while | flops 212767776 | bytes 1912177 | solution.py:42
  173.6 16.5 %while.23 = (s32[]{:T(128)}, f32[53,512]{1,0:T(8,128)S(1)}, s32[]{:T(128)}, s32[4]{0:T(128)S(1)}, f32[4]{0:T(128)S(1)}, /*index=5*/f32[53,512]{1,0:T(8,128)S(1)}...) while((s32[]{:T(128)}, f32[53,512]{1,0:T(8,128)S(1)}, ...), condition=%wide.region_4.4_spmd.clone, body=%wide.region_3.3_spmd.clone.sunk | while | flops 212767776 | bytes 1912177 | solution.py:42
  176.6 0.9 fusion.37
  190.7 1.7 copy.14
  192.4 1.0 reshape.20
  193.4 1.7 copy.15
  195.7 1.9 collective-permute-start.1
  197.6 59.1 %collective-permute-start = (f32[53,1,128]{2,0,1:T(8,128)S(1)}, f32[53,1,128]{2,0,1:T(8,128)S(1)}, u32[]{:S(2)}, u32[]{:S(2)}) collective-permute-start(f32[53,1,128]{2,0,1:T(8,128)S(1)} %get-tuple-element.197), channel_id=1, source_target_pairs={{32,0},{64,32},{96,64},{128,96},{160,128},{192,160},{224,192},{256... | collective-permute-start | bytes 81416 | tf_op jit(solution)/shard_map/ppermute | solution.py:18
  256.7 1.5 collective-permute-done
  258.3 1.3 fusion.19
  259.6 1.6 copy.16
  261.1 1.9 collective-permute-start.2
  263.5 2.4 collective-permute-start.3
  266.3 2.2 collective-permute-done.3
  268.5 1.4 copy.19
  269.9 2.0 fusion.14
  271.9 1.1 copy.20
  (370 shorter events, 129.0 us)
Async XLA Ops:
  0.0 5.4 %copy-start = (f32[53,32,128]{2,1,0:T(8,128)S(1)}, f32[53,32,128]{2,1,0:T(8,128)}, u32[]{:S(2)}) copy-start(f32[53,32,128]{2,1,0:T(8,128)} %param.12) | copy-start | bytes 2605060
  0.0 0.7 copy-start.1
  4.0 0.8 copy-start.3
  7.9 0.9 copy-start.2
  7.9 0.9 copy-start.5
  7.9 0.9 copy-start.6
  7.9 0.9 copy-start.7
  195.7 61.0 %collective-permute-start.1 = (f32[53,1,128]{2,0,1:T(8,128)S(1)}, f32[53,1,128]{2,0,1:T(8,128)S(1)}, u32[]{:S(2)}, u32[]{:S(2)}) collective-permute-start(f32[53,1,128]{2,0,1:T(8,128)S(1)} %get-tuple-element.196), channel_id=1, source_target_pairs={{0,32},{32,64},{64,96},{96,128},{128,160},{160,192},{192,224},{224... | collective-permute-start | bytes 81416 | tf_op jit(solution)/shard_map/ppermute | solution.py:17
  197.6 60.6 %collective-permute-start = (f32[53,1,128]{2,0,1:T(8,128)S(1)}, f32[53,1,128]{2,0,1:T(8,128)S(1)}, u32[]{:S(2)}, u32[]{:S(2)}) collective-permute-start(f32[53,1,128]{2,0,1:T(8,128)S(1)} %get-tuple-element.197), channel_id=1, source_target_pairs={{32,0},{64,32},{96,64},{128,96},{160,128},{192,160},{224,192},{256... | collective-permute-start | bytes 81416 | tf_op jit(solution)/shard_map/ppermute | solution.py:18
  261.1 4.7 %collective-permute-start.2 = (f32[53,34,1]{0,2,1:T(1,128)S(1)}, f32[53,34,1]{0,2,1:T(1,128)S(1)}, u32[]{:S(2)}, u32[]{:S(2)}) collective-permute-start(f32[53,34,1]{0,2,1:T(1,128)S(1)} %copy.16), channel_id=1, source_target_pairs={{1,0},{2,1},{3,2},{4,3},{5,4},{6,5},{7,6},{8,7},{9,8},{10,9},{11,1... | collective-permute-start | bytes 21632 | tf_op jit(solution)/shard_map/ppermute | solution.py:18
  263.5 5.1 %collective-permute-start.3 = (f32[53,34,1]{0,2,1:T(1,128)S(1)}, f32[53,34,1]{0,2,1:T(1,128)S(1)}, u32[]{:S(2)}, u32[]{:S(2)}) collective-permute-start(f32[53,34,1]{0,2,1:T(1,128)S(1)} %copy.18), channel_id=1, source_target_pairs={{0,1},{1,2},{2,3},{3,4},{4,5},{5,6},{6,7},{7,8},{8,9},{9,10},{10,1... | collective-permute-start | bytes 21632 | tf_op jit(solution)/shard_map/ppermute | solution.py:17
  266.3 3.6 %copy-start.4 = (f32[53]{0:T(128)S(1)}, f32[53]{0:T(128)}, u32[]{:S(2)}) copy-start(f32[53]{0:T(128)} %param.19) | copy-start | bytes 640
where the time goes:
time: 277 us; the launch traced here: 273 us
  matrix products  110 us (40%)
  starting transfers between devices  65.3 us (24%)
  loops' own time  52 us (19%)
  local copies, waits for them, and re-layouts  27.8 us (10%)
  other arithmetic  14.2 us (5%)
  waiting for transfers between devices  3.71 us (1%)
    dot_general x73, matrix products, section(): drive = jnp.dot(reactant_orders, current, precision=lax.Precision.HIGHEST)  65.8 us
    ppermute x2, starting transfers between devices, padded_2(): after = lax.ppermute(leading, axis, down)  61 us
    another operation x8, loops' own time, relax_group(): return lax.fori_loop(0, jnp.max(counts_group), section, start_state)  51.8 us
    dot_general x73, matrix products, section(): source = jnp.dot(net_stoich, forward, precision=lax.Precision.HIGHEST)  44 us
  transfers between devices with their start and end apart: 4, of which 2 were waited for; matrix products, arithmetic and copies ran while one was open for 0% of the time, Pallas kernels for 0%

commit v1 on v0

v1 whole, which is shorter than its diff:
```python
import functools

import jax
import jax.numpy as jnp
import numpy as np
from jax import lax
from jax.experimental import pallas as pl
from jax.experimental.pallas import tpu as pltpu
from jax.sharding import PartitionSpec as P

SPECIES = 53
REACTIONS = 325
ROWS = 32
CELLS = 128
MOST = 12
S_PAD = 56
V_PAD = 64
R_PAD = 352
WIDE = ROWS * CELLS
CHUNKS = ROWS // 2
F8_SECTIONS = 9
BF_SECTIONS = 2
UNROLL = 3
LAG = 8
PAIR = 4
ORDER_SCALE = 8.0
STOICH_SCALE = 64.0
RATE_SCALE = 32.0

bf16 = jnp.bfloat16
f8 = jnp.float8_e4m3fn
f32 = jnp.float32
MESH = pl.DeviceIdType.MESH


def step_table():
    table = np.zeros((16, MOST), np.float32)
    for count in range(1, MOST + 1):
        for j in range(count):
            node = np.cos(np.pi * (2 * j + 1) / (2 * count))
            table[count, MOST - count + j] = 1.0 / (4.5 + 3.5 * node)
    return table


def split(value, dtype):
    high = value.astype(dtype)
    return high, (value - high.astype(f32)).astype(dtype)


def dot(left, right):
    return jnp.dot(left, right, preferred_element_type=f32)


def block(b):
    return pl.ds(b * CELLS, CELLS)


def chunk(c):
    return pl.ds(c * 2 * CELLS, 2 * CELLS)


def kernel(
    sec_hbm, tab_hbm, comp_hbm, theta_hbm, orders_hbm, stoich_hbm, prefactor_hbm, activation_hbm,
    diff_hbm, out, sec, tab, comp, theta, orders, stoich, log_prefactor, activation, diffusivity, vs, base, rate, rate_b, f_b, f_8, orders_8, orders_b, stoich_8, stoich_b,
    prefactor_col, activation_col, diff_col, edges, halo, load_sems, send_sems, recv_sems,
):
    gx, gy = lax.axis_index("gx"), lax.axis_index("gy")
    nx, ny = lax.axis_size("gx"), lax.axis_size("gy")
    sides = (
        (gx > 0, (gx - 1, gy)),
        (gx < nx - 1, (gx + 1, gy)),
        (gy > 0, (gx, gy - 1)),
        (gy < ny - 1, (gx, gy + 1)),
    )
    peers = (gx + nx - 1) // nx + (2 * nx - 2 - gx) // nx
    peers = peers + (gy + ny - 1) // ny + (2 * ny - 2 - gy) // ny
    pairs = (
        (theta_hbm, theta),
        (prefactor_hbm, log_prefactor),
        (activation_hbm, activation),
        (stoich_hbm, stoich),
        (orders_hbm, orders),
        (diff_hbm, diffusivity),
        (sec_hbm, sec),
        (tab_hbm, tab),
        (comp_hbm, comp),
    )
    loads = [pltpu.make_async_copy(a, b, load_sems.at[i]) for i, (a, b) in enumerate(pairs)]
    for load in loads:
        load.start()
    barrier = pltpu.get_barrier_semaphore()
    for there, device in sides:

        @pl.when(there)
        def _(device=device):
            pl.semaphore_signal(barrier, inc=1, device_id=device, device_id_type=MESH)

    for k, (there, _) in enumerate(sides):

        @pl.when(jnp.logical_not(there))
        def _(k=k):
            halo[k] = jnp.zeros((S_PAD, CELLS), f32)

    for load in loads[:-1]:
        load.wait()
    orders_f = jnp.concatenate([orders[...] * 0.5, jnp.zeros((V_PAD - SPECIES, REACTIONS), f32)], 0)
    orders_f = jnp.concatenate([orders_f, jnp.zeros((V_PAD, 384 - REACTIONS), f32)], 1)
    orders_f = jnp.transpose(orders_f)[:R_PAD]
    high, low = split(orders_f, bf16)
    orders_b[...] = jnp.concatenate([high, high, low], 1)
    high, low = split(orders_f * ORDER_SCALE, f8)
    orders_8[...] = jnp.concatenate([high, high, low, low], 1)
    stoich_f = jnp.concatenate([stoich[...] * 0.5, jnp.zeros((V_PAD - SPECIES, REACTIONS), f32)], 0)
    stoich_f = jnp.concatenate([stoich_f, jnp.zeros((V_PAD, R_PAD - REACTIONS), f32)], 1)
    high, low = split(stoich_f * (1.0 / RATE_SCALE), bf16)
    stoich_b[...] = jnp.concatenate([high, low], 0)
    stoich_8[...] = (stoich_f * STOICH_SCALE).astype(f8)
    rows = [log_prefactor[...].reshape(1, REACTIONS), activation[...].reshape(1, REACTIONS)]
    rows = jnp.concatenate(rows + [jnp.zeros((6, REACTIONS), f32)], 0)
    rows = jnp.concatenate([rows, jnp.zeros((8, 384 - REACTIONS), f32)], 1)
    columns = jnp.transpose(rows)
    prefactor_col[...] = jnp.broadcast_to(columns[:R_PAD, 0:1], (R_PAD, CELLS))
    activation_col[...] = jnp.broadcast_to(columns[:R_PAD, 1:2], (R_PAD, CELLS))
    rows = jnp.concatenate([diffusivity[...], jnp.zeros((1, CELLS - SPECIES), f32)], 1)
    rows = jnp.concatenate([rows, jnp.zeros((7, CELLS), f32)], 0)
    diff_col[...] = jnp.broadcast_to(jnp.transpose(rows)[:S_PAD, 0:1], (S_PAD, CELLS))

    for b in range(ROWS):
        r = jnp.exp(prefactor_col[...] - activation_col[...] * theta[b : b + 1, :]) * RATE_SCALE
        rate[:, block(b)] = r
        rate_b[:, block(b)] = r.astype(bf16)

    loads[-1].wait()

    def start_of(b):
        value = comp[pl.ds(b, SPECIES, stride=ROWS), :]
        return jnp.concatenate([value, jnp.zeros((S_PAD - SPECIES, CELLS), f32)], 0)

    vs[S_PAD:, :] = jnp.zeros((V_PAD - S_PAD, WIDE), f32)
    for c in range(CHUNKS):
        for b in (2 * c, 2 * c + 1):
            vs[0:S_PAD, block(b)] = start_of(b)
        bias = dot(stoich_b[0:S_PAD, :], rate_b[:, chunk(c)])
        base[:, chunk(c)] = vs[0:S_PAD, chunk(c)] + bias

    def forward_f8(c):
        high, low = split(vs[:, chunk(c)] * (1.0 / ORDER_SCALE), f8)
        drive = dot(orders_8[...], jnp.concatenate([high, low, high, low], 0))
        f_8[:, chunk(c)] = (jnp.tanh(drive.astype(bf16)) * rate_b[:, chunk(c)]).astype(f8)

    def forward_bf(c):
        drive = dot(orders_b[:, 0:V_PAD], vs[:, chunk(c)].astype(bf16))
        f_b[:, chunk(c)] = (jnp.tanh(drive) * rate[:, chunk(c)]).astype(bf16)

    def update(c, j, target):
        for h in range(2):
            b = 2 * c + h
            step = tab[sec[0, b], j]
            v = vs[0:S_PAD, block(b)]
            vs[0:S_PAD, block(b)] = v + step * (target[:, h * CELLS : (h + 1) * CELLS] - v)

    def relax_f8(c, j):
        product = dot(stoich_8[...], f_8[:, chunk(c)])[0:S_PAD]
        update(c, j, base[:, chunk(c)] + product * (1.0 / (STOICH_SCALE * RATE_SCALE)))

    def relax_bf(c, j):
        update(c, j, base[:, chunk(c)] + dot(stoich_b[0:S_PAD, :], f_b[:, chunk(c)]))

    def section(j, forward, relax):
        for first in range(0, CHUNKS + LAG, PAIR):
            for c in range(first, first + PAIR):
                if c < CHUNKS:
                    forward(c)
            for c in range(first, first + PAIR):
                if LAG <= c:
                    relax(c - LAG, j)

    def sections_f8(i, _):
        for u in range(UNROLL):
            section(i * UNROLL + u, forward_f8, relax_f8)
        return 0

    lax.fori_loop(0, F8_SECTIONS // UNROLL, sections_f8, 0)
    for j in range(F8_SECTIONS, F8_SECTIONS + BF_SECTIONS):
        section(j, forward_bf, relax_bf)

    def last_section(c):
        high, low = split(vs[:, chunk(c)], bf16)
        drive = dot(orders_b[...], jnp.concatenate([high, low, high], 0))
        r = rate[:, chunk(c)]
        high, low = split(r + r * jnp.tanh(drive), bf16)
        product = dot(stoich_b[...], high)
        source = product[0:S_PAD] + product[V_PAD : V_PAD + S_PAD] + dot(stoich_b[0:S_PAD, :], low)
        start = jnp.concatenate([start_of(2 * c), start_of(2 * c + 1)], 1)
        update(c, MOST - 1, start + source)

    def send(k, source):
        return pltpu.make_async_remote_copy(
            src_ref=source,
            dst_ref=halo.at[k ^ 1],
            send_sem=send_sems.at[k],
            recv_sem=recv_sems.at[k],
            device_id=sides[k][1],
            device_id_type=MESH,
        )

    copies = [
        send(0, vs.at[0:S_PAD, block(0)]),
        send(1, vs.at[0:S_PAD, block(ROWS - 1)]),
        send(2, edges),
        send(3, edges),
    ]

    last_section(0)
    last_section(CHUNKS - 1)
    pl.semaphore_wait(barrier, peers)
    for k in (0, 1):

        @pl.when(sides[k][0])
        def _(k=k):
            copies[k].start()

    for c in range(1, CHUNKS - 1):
        last_section(c)

    lane = lax.broadcasted_iota(jnp.int32, (S_PAD, CELLS), 1)
    packed = jnp.zeros((S_PAD, CELLS), f32)
    for b in range(ROWS):
        v = vs[0:S_PAD, block(b)]
        packed = jnp.where(lane == b, pltpu.roll(v, b, 1), packed)
        packed = jnp.where(lane == 64 + b, pltpu.roll(v, (64 + b + 1) % CELLS, 1), packed)
    edges[...] = packed
    for k in (2, 3):

        @pl.when(sides[k][0])
        def _(k=k):
            copies[k].start()

    d = diff_col[...]
    for b in range(ROWS):
        v = vs[0:S_PAD, block(b)]
        total = jnp.where(lane == 0, 0.0, pltpu.roll(v, 1, 1)) - 4.0 * v
        total = total + jnp.where(lane == CELLS - 1, 0.0, pltpu.roll(v, CELLS - 1, 1))
        if b > 0:
            total = total + vs[0:S_PAD, block(b - 1)]
        if b < ROWS - 1:
            total = total + vs[0:S_PAD, block(b + 1)]
        base[:, block(b)] = v + d * total

    for k, (there, _) in enumerate(sides):

        @pl.when(there)
        def _(k=k):
            copies[k].wait_send()
            copies[k ^ 1].wait_recv()

    before, after = halo[2], halo[3]
    for b in range(ROWS):
        total = jnp.where(lane == 0, pltpu.roll(before, (CELLS - 64 - b) % CELLS, 1), 0.0)
        total = total + jnp.where(lane == CELLS - 1, pltpu.roll(after, CELLS - 1 - b, 1), 0.0)
        if b == 0:
            total = total + halo[0]
        if b == ROWS - 1:
            total = total + halo[1]
        result = base[:, block(b)] + d * total
        out[pl.ds(b, SPECIES, stride=ROWS), :] = result[0:SPECIES]


def body(
    composition,
    inverse_temp,
    sections,
    reactant_orders,
    net_stoich,
    log_prefactor,
    activation,
    diffusivity,
):
    scratch = pltpu.VMEM
    operands = (
        sections.reshape(1, ROWS),
        jnp.asarray(step_table()),
        composition.reshape(SPECIES * ROWS, CELLS),
        inverse_temp,
        reactant_orders.T,
        net_stoich,
        log_prefactor,
        activation,
        diffusivity.reshape(1, SPECIES),
    )
    operands = [pltpu.with_memory_space_constraint(x, pltpu.HBM) for x in operands]
    result = pl.pallas_call(
        kernel,
        out_shape=scratch((SPECIES * ROWS, CELLS), f32),
        in_specs=[pl.BlockSpec(memory_space=pltpu.HBM)] * 9,
        out_specs=pl.BlockSpec(memory_space=pltpu.VMEM),
        scratch_shapes=[
            pltpu.SMEM((1, ROWS), jnp.int32),
            pltpu.SMEM((16, MOST), f32),
            scratch((SPECIES * ROWS, CELLS), f32),
            scratch((ROWS, CELLS), f32),
            scratch((SPECIES, REACTIONS), f32),
            scratch((SPECIES, REACTIONS), f32),
            scratch((REACTIONS,), f32),
            scratch((REACTIONS,), f32),
            scratch((1, SPECIES), f32),
            scratch((V_PAD, WIDE), f32),
            scratch((S_PAD, WIDE), f32),
            scratch((R_PAD, WIDE), f32),
            scratch((R_PAD, WIDE), bf16),
            scratch((R_PAD, WIDE), bf16),
            scratch((R_PAD, WIDE), f8),
            scratch((R_PAD, 4 * V_PAD), f8),
            scratch((R_PAD, 3 * V_PAD), bf16),
            scratch((V_PAD, R_PAD), f8),
            scratch((2 * V_PAD, R_PAD), bf16),
            scratch((R_PAD, CELLS), f32),
            scratch((R_PAD, CELLS), f32),
            scratch((S_PAD, CELLS), f32),
            scratch((S_PAD, CELLS), f32),
            scratch((4, S_PAD, CELLS), f32),
            pltpu.SemaphoreType.DMA((9,)),
            pltpu.SemaphoreType.DMA((4,)),
            pltpu.SemaphoreType.DMA((4,)),
        ],
        compiler_params=pltpu.CompilerParams(
            collective_id=0, has_side_effects=True, vmem_limit_bytes=48 << 20
        ),
    )(*operands)
    return result.reshape(SPECIES, ROWS, CELLS)


def solution(mesh):
    return jax.shard_map(
        body,
        mesh=mesh,
        in_specs=(P(None, "gx", "gy"), P("gx", "gy"), P("gx", "gy"), P(), P(), P(), P(), P()),
        out_specs=P(None, "gx", "gy"),
        check_vma=False,
    )
```

time: 277 us -> 36.6 us (0.13)
  the two profiles are of different devices: /device:TPU:110 before, /device:TPU:1 now
where the time goes in v1:
time: 36.6 us; the launch traced here: 36.4 us
  Pallas kernels  35.5 us (97%)
  local copies, waits for them, and re-layouts  0.91 us (2%)
    pallas_call x1, Pallas kernels, body(): pl.pallas_call(kernel, out_shape=scratch((SPECIES * ROWS, CELLS), f32), i...  35.5 us
    unnamed x1, local copies, waits for them, and re-layouts  0.91 us

profile of v1, /device:TPU:1, one launch (start us, length us, event | category | flops | bytes accessed | tf_op | source)
XLA Modules:
  0.0 36.4 jit_solution(16259311815566327899)
XLA Ops:
  0.0 35.5 %shard_map.91 = f32[1696,128]{1,0:T(8,128)S(1)} custom-call(s32[1,32]{1,0:T(1,128)} %bitcast.8, f32[16,12]{1,0:T(8,128)} %constant.2.clone.tab_hbm, f32[1696,128]{1,0:T(8,128)} %bitcast.6, f32[32,128]{1,0:T(8,128)} %theta_hbm.1, f32[53,325]{1,0:T(8,128)} %bitcast.7, f32[53,325]{1,0:T(8,128)} %stoich_hbm.1, f32[325]{0:T(512)} %prefactor_hbm.1, ...), custom_call_target="tpu_custom_call" | custom-call | tf_op jit(solution)/shard_map/pallas_call | solution.py:292
  35.5 0.9 %copy.11 = f32[53,32,128]{2,1,0:T(8,128)} copy(f32[53,32,128]{2,1,0:T(8,128)S(1)} %bitcast.5) | data formatting | bytes 1736704

commit v2 on v1

v2 whole, which is shorter than its diff:
```python
import functools

import jax
import jax.numpy as jnp
import numpy as np
from jax import lax
from jax.experimental import pallas as pl
from jax.experimental.pallas import tpu as pltpu
from jax.sharding import PartitionSpec as P

SPECIES = 53
REACTIONS = 325
ROWS = 32
CELLS = 128
MOST = 12
S_PAD = 56
V_PAD = 64
R_PAD = 352
HALO = 3
WIDE = (ROWS + HALO) * CELLS
CHUNKS = ROWS // 2
EARLY = tuple(range(12))
LATE = tuple(range(12, CHUNKS + 2))
F8_SECTIONS = 9
BF_SECTIONS = 2
UNROLL = 3
LAG = 8
PACKET = S_PAD + 8
PAIR = 4
ORDER_SCALE = 8.0
STOICH_SCALE = 64.0
RATE_SCALE = 32.0

bf16 = jnp.bfloat16
f8 = jnp.float8_e4m3fn
f32 = jnp.float32
MESH = pl.DeviceIdType.MESH


def step_table():
    table = np.zeros((16, MOST), np.float32)
    for count in range(1, MOST + 1):
        for j in range(count):
            node = np.cos(np.pi * (2 * j + 1) / (2 * count))
            table[count, MOST - count + j] = 1.0 / (4.5 + 3.5 * node)
    return table


def split(value, dtype):
    high = value.astype(dtype)
    return high, (value - high.astype(f32)).astype(dtype)


def dot(left, right):
    return jnp.dot(left, right, preferred_element_type=f32)


def block(b):
    return pl.ds(b * CELLS, CELLS)


def blocks_of(c):
    return tuple(b for b in (2 * c, 2 * c + 1) if b < ROWS + HALO)


def chunk(c):
    return pl.ds(c * 2 * CELLS, len(blocks_of(c)) * CELLS)


def kernel(
    sec_hbm, tab_hbm, steps_hbm, comp_hbm, theta_hbm, orders_hbm, stoich_hbm, prefactor_hbm,
    activation_hbm, diff_hbm, out, sec, tab, counts, steps, comp, theta, orders, stoich,
    log_prefactor, activation, diffusivity, vs, base, rate, rate_b, f_b, f_8, orders_8, orders_b,
    stoich_8, stoich_b, prefactor_col, activation_col, diff_col, packets, halo, halo_start,
    halo_steps, load_sems, send_sems, recv_sems,
):
    gx, gy = lax.axis_index("gx"), lax.axis_index("gy")
    nx, ny = lax.axis_size("gx"), lax.axis_size("gy")
    sides = (
        (gx > 0, (gx - 1, gy)),
        (gx < nx - 1, (gx + 1, gy)),
        (gy > 0, (gx, gy - 1)),
        (gy < ny - 1, (gx, gy + 1)),
    )
    peers = (gx + nx - 1) // nx + (2 * nx - 2 - gx) // nx
    peers = peers + (gy + ny - 1) // ny + (2 * ny - 2 - gy) // ny
    next_to_first = 1 - (gx + gy + nx + ny - 2) // (nx + ny) - (1 - (gx + gy + nx + ny - 1) // (nx + ny))
    far = 1 - (gx % 4 + 3) // 4
    far = jnp.maximum(far * ((gx + nx - 1) // nx), (gy % 16) // 15 * ((2 * ny - 2 - gy) // ny))
    turn = far + (2 - far) * next_to_first

    pairs = (
        (comp_hbm, comp),
        (theta_hbm, theta),
        (sec_hbm, sec),
        (sec_hbm, counts),
        (prefactor_hbm, log_prefactor),
        (activation_hbm, activation),
        (stoich_hbm, stoich),
        (orders_hbm, orders),
        (diff_hbm, diffusivity),
        (tab_hbm, tab),
        (steps_hbm, steps),
    )
    loads = [pltpu.make_async_copy(a, b, load_sems.at[i]) for i, (a, b) in enumerate(pairs)]
    for load in loads:
        load.start()
    barrier = pltpu.get_barrier_semaphore()
    for there, device in sides:

        @pl.when(there)
        def _(device=device):
            pl.semaphore_signal(barrier, inc=1, device_id=device, device_id_type=MESH)

    for k, (there, _) in enumerate(sides):

        @pl.when(jnp.logical_not(there))
        def _(k=k):
            halo[k] = jnp.zeros((PACKET, CELLS), f32)

    copies = [
        pltpu.make_async_remote_copy(
            src_ref=packets.at[min(k, 2)],
            dst_ref=halo.at[k ^ 1],
            send_sem=send_sems.at[k],
            recv_sem=recv_sems.at[k],
            device_id=sides[k][1],
            device_id_type=MESH,
        )
        for k in range(4)
    ]

    def send_at(point):
        @pl.when(turn == point)
        def _():
            pl.semaphore_wait(barrier, peers)
            for k, (there, _) in enumerate(sides):

                @pl.when(there)
                def _(k=k):
                    copies[k].start()

    for load in loads[1:]:
        load.wait()
    orders_f = jnp.concatenate([orders[...] * 0.5, jnp.zeros((V_PAD - SPECIES, REACTIONS), f32)], 0)
    orders_f = jnp.concatenate([orders_f, jnp.zeros((V_PAD, 384 - REACTIONS), f32)], 1)
    orders_f = jnp.transpose(orders_f)[:R_PAD]
    high, low = split(orders_f, bf16)
    orders_b[...] = jnp.concatenate([high, high, low], 1)
    high, low = split(orders_f * ORDER_SCALE, f8)
    orders_8[...] = jnp.concatenate([high, high, low, low], 1)
    stoich_f = jnp.concatenate([stoich[...] * 0.5, jnp.zeros((V_PAD - SPECIES, REACTIONS), f32)], 0)
    stoich_f = jnp.concatenate([stoich_f, jnp.zeros((V_PAD, R_PAD - REACTIONS), f32)], 1)
    high, low = split(stoich_f * (1.0 / RATE_SCALE), bf16)
    stoich_b[...] = jnp.concatenate([high, low], 0)
    stoich_8[...] = (stoich_f * STOICH_SCALE).astype(f8)
    rows = [log_prefactor[...].reshape(1, REACTIONS), activation[...].reshape(1, REACTIONS)]
    rows = jnp.concatenate(rows + [jnp.zeros((6, REACTIONS), f32)], 0)
    rows = jnp.concatenate([rows, jnp.zeros((8, 384 - REACTIONS), f32)], 1)
    columns = jnp.transpose(rows)
    prefactor_col[...] = jnp.broadcast_to(columns[:R_PAD, 0:1], (R_PAD, CELLS))
    activation_col[...] = jnp.broadcast_to(columns[:R_PAD, 1:2], (R_PAD, CELLS))
    rows = jnp.concatenate([diffusivity[...], jnp.zeros((1, CELLS - SPECIES), f32)], 1)
    rows = jnp.concatenate([rows, jnp.zeros((7, CELLS), f32)], 0)
    diff_col[...] = jnp.broadcast_to(jnp.transpose(rows)[:S_PAD, 0:1], (S_PAD, CELLS))

    lane = lax.broadcasted_iota(jnp.int32, (S_PAD, CELLS), 1)
    rest = jnp.zeros((6, CELLS), f32)
    loads[0].wait()

    def start_of(b):
        if b >= ROWS:
            return halo_start[:, block(b - ROWS)]
        value = comp[pl.ds(b, SPECIES, stride=ROWS), :]
        return jnp.concatenate([value, jnp.zeros((S_PAD - SPECIES, CELLS), f32)], 0)

    vs[S_PAD:, :] = jnp.zeros((V_PAD - S_PAD, WIDE), f32)
    packed = jnp.zeros((S_PAD, CELLS), f32)
    for b in range(ROWS):
        v = start_of(b)
        vs[0:S_PAD, block(b)] = v
        packed = jnp.where(lane == b, pltpu.roll(v, b, 1), packed)
        packed = jnp.where(lane == 64 + b, pltpu.roll(v, (64 + b + 1) % CELLS, 1), packed)
        if b in (0, ROWS - 1):
            count = jnp.full((1, CELLS), sec[0, b].astype(f32))
            tail = jnp.concatenate([theta[b : b + 1, :], count, rest], 0)
            packets[b // (ROWS - 1)] = jnp.concatenate([v, tail], 0)
    temps = jnp.concatenate([theta[...], jnp.zeros((CELLS - ROWS, CELLS), f32)], 0)
    temps = jnp.transpose(temps)
    temps = temps[0:1, :] + pltpu.roll(temps[CELLS - 8 : CELLS, :], 64, 1)[7:8, :]
    count = jnp.concatenate([counts[...].astype(f32), jnp.zeros((1, CELLS - ROWS), f32)], 1)
    count = jnp.broadcast_to(count, (8, CELLS))
    count = (count + pltpu.roll(count, 64, 1))[0:1, :]
    packets[2] = jnp.concatenate([packed, temps, count, rest], 0)

    send_at(0)

    def set_rate(b, temp):
        r = jnp.exp(prefactor_col[...] - activation_col[...] * temp) * RATE_SCALE
        rate[:, block(b)] = r
        rate_b[:, block(b)] = r.astype(bf16)

    def set_base(c):
        bias = dot(stoich_b[0:S_PAD, :], rate_b[:, chunk(c)])
        base[:, chunk(c)] = vs[0:S_PAD, chunk(c)] + bias

    for c in range(CHUNKS):
        for b in blocks_of(c):
            set_rate(b, theta[b : b + 1, :])
        set_base(c)

    def forward_f8(c):
        high, low = split(vs[:, chunk(c)] * (1.0 / ORDER_SCALE), f8)
        drive = dot(orders_8[...], jnp.concatenate([high, low, high, low], 0))
        f_8[:, chunk(c)] = (jnp.tanh(drive.astype(bf16)) * rate_b[:, chunk(c)]).astype(f8)

    def forward_bf(c):
        drive = dot(orders_b[:, 0:V_PAD], vs[:, chunk(c)].astype(bf16))
        f_b[:, chunk(c)] = (jnp.tanh(drive) * rate[:, chunk(c)]).astype(bf16)

    def update(c, j, target):
        for h, b in enumerate(blocks_of(c)):
            if b < ROWS:
                step = tab[sec[0, b], j]
            else:
                step = halo_steps[j, :, block(b - ROWS)][0:1]
            v = vs[0:S_PAD, block(b)]
            vs[0:S_PAD, block(b)] = v + step * (target[:, h * CELLS : (h + 1) * CELLS] - v)

    def relax_f8(c, j):
        product = dot(stoich_8[...], f_8[:, chunk(c)])[0:S_PAD]
        update(c, j, base[:, chunk(c)] + product * (1.0 / (STOICH_SCALE * RATE_SCALE)))

    def relax_bf(c, j):
        update(c, j, base[:, chunk(c)] + dot(stoich_b[0:S_PAD, :], f_b[:, chunk(c)]))

    def section(chunks, j, forward, relax):
        for first in range(0, len(chunks) + LAG, PAIR):
            for at in range(first, first + PAIR):
                if at < len(chunks):
                    forward(chunks[at])
            for at in range(first, first + PAIR):
                if LAG <= at < len(chunks) + LAG:
                    relax(chunks[at - LAG], j)

    def sections_f8(chunks):
        def some(i, _):
            for u in range(UNROLL):
                section(chunks, i * UNROLL + u, forward_f8, relax_f8)
            return 0

        lax.fori_loop(0, F8_SECTIONS // UNROLL, some, 0)

    def sections_bf(chunks):
        for j in range(F8_SECTIONS, F8_SECTIONS + BF_SECTIONS):
            section(chunks, j, forward_bf, relax_bf)

    def last_section(c):
        high, low = split(vs[:, chunk(c)], bf16)
        drive = dot(orders_b[...], jnp.concatenate([high, low, high], 0))
        r = rate[:, chunk(c)]
        high, low = split(r + r * jnp.tanh(drive), bf16)
        product = dot(stoich_b[...], high)
        source = product[0:S_PAD] + product[V_PAD : V_PAD + S_PAD] + dot(stoich_b[0:S_PAD, :], low)
        start = [start_of(b) for b in blocks_of(c)]
        start = jnp.concatenate(start, 1) if len(start) > 1 else start[0]
        update(c, MOST - 1, start + source)

    sections_f8(EARLY)
    send_at(1)
    sections_bf(EARLY)
    for c in EARLY:
        last_section(c)
    send_at(2)

    for k, (there, _) in enumerate(sides):

        @pl.when(there)
        def _(k=k):
            copies[k ^ 1].wait_recv()

    side = lax.broadcasted_iota(jnp.int32, (PACKET, CELLS), 1) < 64
    which = lax.broadcasted_iota(jnp.int32, (16, CELLS), 0).astype(f32)
    for q in range(HALO):
        packet = halo[q] if q < 2 else jnp.where(side, halo[3], halo[2])
        halo_start[:, block(q)] = packet[0:S_PAD]
        vs[0:S_PAD, block(ROWS + q)] = packet[0:S_PAD]
        count = jnp.broadcast_to(packet[S_PAD + 1 : S_PAD + 2], (16, CELLS))
        found = jnp.dot(
            steps[...],
            jnp.where(count == which, 1.0, 0.0),
            precision=lax.Precision.HIGHEST,
            preferred_element_type=f32,
        )
        for j in range(MOST):
            halo_steps[j, :, block(q)] = jnp.broadcast_to(found[j : j + 1], (8, CELLS))
        set_rate(ROWS + q, packet[S_PAD : S_PAD + 1])
    for c in range(CHUNKS, CHUNKS + 2):
        set_base(c)

    sections_f8(LATE)
    sections_bf(LATE)
    for c in LATE:
        last_section(c)

    d = diff_col[...]
    columns = vs[0:S_PAD, block(ROWS + 2)]
    for b in range(ROWS):
        v = vs[0:S_PAD, block(b)]
        above = vs[0:S_PAD, block(b - 1 if b > 0 else ROWS)]
        below = vs[0:S_PAD, block(b + 1 if b < ROWS - 1 else ROWS + 1)]
        before = pltpu.roll(columns, (CELLS - 64 - b) % CELLS, 1)
        before = jnp.where(lane == 0, before, pltpu.roll(v, 1, 1))
        after = pltpu.roll(columns, CELLS - 1 - b, 1)
        after = jnp.where(lane == CELLS - 1, after, pltpu.roll(v, CELLS - 1, 1))
        result = v + d * (above + below + before + after - 4.0 * v)
        out[pl.ds(b, SPECIES, stride=ROWS), :] = result[0:SPECIES]

    for k, (there, _) in enumerate(sides):

        @pl.when(there)
        def _(k=k):
            copies[k].wait_send()


def body(
    composition,
    inverse_temp,
    sections,
    reactant_orders,
    net_stoich,
    log_prefactor,
    activation,
    diffusivity,
):
    scratch = pltpu.VMEM
    operands = (
        sections.reshape(1, ROWS),
        jnp.asarray(step_table()),
        jnp.asarray(np.pad(step_table().T, ((0, 4), (0, 0)))),
        composition.reshape(SPECIES * ROWS, CELLS),
        inverse_temp,
        reactant_orders.T,
        net_stoich,
        log_prefactor,
        activation,
        diffusivity.reshape(1, SPECIES),
    )
    operands = [pltpu.with_memory_space_constraint(x, pltpu.HBM) for x in operands]
    result = pl.pallas_call(
        kernel,
        out_shape=scratch((SPECIES * ROWS, CELLS), f32),
        in_specs=[pl.BlockSpec(memory_space=pltpu.HBM)] * 10,
        out_specs=pl.BlockSpec(memory_space=pltpu.VMEM),
        scratch_shapes=[
            pltpu.SMEM((1, ROWS), jnp.int32),
            pltpu.SMEM((16, MOST), f32),
            scratch((1, ROWS), jnp.int32),
            scratch((16, 16), f32),
            scratch((SPECIES * ROWS, CELLS), f32),
            scratch((ROWS, CELLS), f32),
            scratch((SPECIES, REACTIONS), f32),
            scratch((SPECIES, REACTIONS), f32),
            scratch((REACTIONS,), f32),
            scratch((REACTIONS,), f32),
            scratch((1, SPECIES), f32),
            scratch((V_PAD, WIDE), f32),
            scratch((S_PAD, WIDE), f32),
            scratch((R_PAD, WIDE), f32),
            scratch((R_PAD, WIDE), bf16),
            scratch((R_PAD, WIDE), bf16),
            scratch((R_PAD, WIDE), f8),
            scratch((R_PAD, 4 * V_PAD), f8),
            scratch((R_PAD, 3 * V_PAD), bf16),
            scratch((V_PAD, R_PAD), f8),
            scratch((2 * V_PAD, R_PAD), bf16),
            scratch((R_PAD, CELLS), f32),
            scratch((R_PAD, CELLS), f32),
            scratch((S_PAD, CELLS), f32),
            scratch((3, PACKET, CELLS), f32),
            scratch((4, PACKET, CELLS), f32),
            scratch((S_PAD, HALO * CELLS), f32),
            scratch((MOST, 8, HALO * CELLS), f32),
            pltpu.SemaphoreType.DMA((11,)),
            pltpu.SemaphoreType.DMA((4,)),
            pltpu.SemaphoreType.DMA((4,)),
        ],
        compiler_params=pltpu.CompilerParams(
            collective_id=0, has_side_effects=True, vmem_limit_bytes=48 << 20
        ),
    )(*operands)
    return result.reshape(SPECIES, ROWS, CELLS)


def solution(mesh):
    return jax.shard_map(
        body,
        mesh=mesh,
        in_specs=(P(None, "gx", "gy"), P("gx", "gy"), P("gx", "gy"), P(), P(), P(), P(), P()),
        out_specs=P(None, "gx", "gy"),
        check_vma=False,
    )
```

time: 36.6 us -> 34 us (0.929)
  the two profiles are of different devices: /device:TPU:1 before, /device:TPU:119 now
where the time goes in v2:
time: 34 us; the launch traced here: 33.8 us
  Pallas kernels  32.9 us (97%)
  local copies, waits for them, and re-layouts  0.91 us (3%)
    pallas_call x1, Pallas kernels, body(): pl.pallas_call(kernel, out_shape=scratch((SPECIES * ROWS, CELLS), f32), i...  32.9 us
    unnamed x1, local copies, waits for them, and re-layouts  0.91 us

profile of v2, /device:TPU:119, one launch (start us, length us, event | category | flops | bytes accessed | tf_op | source)
XLA Modules:
  0.0 33.8 jit_solution(6792806755978547148)
XLA Ops:
  0.0 32.9 %shard_map.100 = f32[1696,128]{1,0:T(8,128)S(1)} custom-call(s32[1,32]{1,0:T(1,128)} %bitcast.8, f32[16,12]{1,0:T(8,128)} %constant.4.clone.tab_hbm, f32[16,16]{1,0:T(8,128)} %constant.5.clone.steps_hbm, f32[1696,128]{1,0:T(8,128)} %bitcast.6, f32[32,128]{1,0:T(8,128)} %theta_hbm.1, f32[53,325]{1,0:T(8,128)} %bitcast.7, f32[53,325]{1,0:T(8,128)} %stoich_hbm.1, ...), custom_call_target="tpu_custom_call" | custom-call | tf_op jit(solution)/shard_map/pallas_call | solution.py:350
  32.9 0.9 %copy.12 = f32[53,32,128]{2,1,0:T(8,128)} copy(f32[53,32,128]{2,1,0:T(8,128)S(1)} %bitcast.5) | data formatting | bytes 1736704

commit v3 on v2

--- a/solution.py
+++ b/solution.py
@@ -24,7 +24,7 @@
 F8_SECTIONS = 9
 BF_SECTIONS = 2
 UNROLL = 3
-LAG = 8
+LAG = 4
 PACKET = S_PAD + 8
 PAIR = 4
 ORDER_SCALE = 8.0
@@ -84,10 +84,12 @@
     )
     peers = (gx + nx - 1) // nx + (2 * nx - 2 - gx) // nx
     peers = peers + (gy + ny - 1) // ny + (2 * ny - 2 - gy) // ny
-    next_to_first = 1 - (gx + gy + nx + ny - 2) // (nx + ny) - (1 - (gx + gy + nx + ny - 1) // (nx + ny))
-    far = 1 - (gx % 4 + 3) // 4
-    far = jnp.maximum(far * ((gx + nx - 1) // nx), (gy % 16) // 15 * ((2 * ny - 2 - gy) // ny))
-    turn = far + (2 - far) * next_to_first
+    next_to_first = 1 - (gx + gy + nx + ny - 2) // (nx + ny)
+    next_to_first = next_to_first - (1 - (gx + gy + nx + ny - 1) // (nx + ny))
+    inner, upper = gx % 4, gy // 16
+    row_far = (1 - (inner + 3) // 4) * ((gx + nx - 1) // nx) * (2 - jnp.minimum(upper, 1))
+    column_far = (gy % 16) // 15 * ((2 * ny - 2 - gy) // ny) * (2 - inner // 2)
+    turn = jnp.maximum(jnp.maximum(row_far, column_far), 3 * next_to_first)
 
     pairs = (
         (comp_hbm, comp),
@@ -147,8 +149,7 @@
     orders_f = jnp.transpose(orders_f)[:R_PAD]
     high, low = split(orders_f, bf16)
     orders_b[...] = jnp.concatenate([high, high, low], 1)
-    high, low = split(orders_f * ORDER_SCALE, f8)
-    orders_8[...] = jnp.concatenate([high, high, low, low], 1)
+    orders_8[...] = (orders_f * ORDER_SCALE).astype(f8)
     stoich_f = jnp.concatenate([stoich[...] * 0.5, jnp.zeros((V_PAD - SPECIES, REACTIONS), f32)], 0)
     stoich_f = jnp.concatenate([stoich_f, jnp.zeros((V_PAD, R_PAD - REACTIONS), f32)], 1)
     high, low = split(stoich_f * (1.0 / RATE_SCALE), bf16)
@@ -209,9 +210,10 @@
             set_rate(b, theta[b : b + 1, :])
         set_base(c)
 
+    send_at(1)
+
     def forward_f8(c):
-        high, low = split(vs[:, chunk(c)] * (1.0 / ORDER_SCALE), f8)
-        drive = dot(orders_8[...], jnp.concatenate([high, low, high, low], 0))
+        drive = dot(orders_8[...], (vs[:, chunk(c)] * (1.0 / ORDER_SCALE)).astype(f8))
         f_8[:, chunk(c)] = (jnp.tanh(drive.astype(bf16)) * rate_b[:, chunk(c)]).astype(f8)
 
     def forward_bf(c):
@@ -243,13 +245,13 @@
                 if LAG <= at < len(chunks) + LAG:
                     relax(chunks[at - LAG], j)
 
-    def sections_f8(chunks):
+    def sections_f8(chunks, start, end):
         def some(i, _):
             for u in range(UNROLL):
                 section(chunks, i * UNROLL + u, forward_f8, relax_f8)
             return 0
 
-        lax.fori_loop(0, F8_SECTIONS // UNROLL, some, 0)
+        lax.fori_loop(start // UNROLL, end // UNROLL, some, 0)
 
     def sections_bf(chunks):
         for j in range(F8_SECTIONS, F8_SECTIONS + BF_SECTIONS):
@@ -266,12 +268,13 @@
         start = jnp.concatenate(start, 1) if len(start) > 1 else start[0]
         update(c, MOST - 1, start + source)
 
-    sections_f8(EARLY)
-    send_at(1)
+    sections_f8(EARLY, 0, 3)
+    send_at(2)
+    sections_f8(EARLY, 3, F8_SECTIONS)
     sections_bf(EARLY)
     for c in EARLY:
         last_section(c)
-    send_at(2)
+    send_at(3)
 
     for k, (there, _) in enumerate(sides):
 
@@ -298,7 +301,7 @@
     for c in range(CHUNKS, CHUNKS + 2):
         set_base(c)
 
-    sections_f8(LATE)
+    sections_f8(LATE, 0, F8_SECTIONS)
     sections_bf(LATE)
     for c in LATE:
         last_section(c)
@@ -370,7 +373,7 @@
             scratch((R_PAD, WIDE), bf16),
             scratch((R_PAD, WIDE), bf16),
             scratch((R_PAD, WIDE), f8),
-            scratch((R_PAD, 4 * V_PAD), f8),
+            scratch((R_PAD, V_PAD), f8),
             scratch((R_PAD, 3 * V_PAD), bf16),
             scratch((V_PAD, R_PAD), f8),
             scratch((2 * V_PAD, R_PAD), bf16),

time: 34 us -> 30 us (0.88)
  the two profiles are of different devices: /device:TPU:119 before, /device:TPU:381 now
where the time goes in v3:
time: 30 us; the launch traced here: 29.8 us
  Pallas kernels  28.9 us (96%)
  local copies, waits for them, and re-layouts  0.91 us (3%)
    pallas_call x1, Pallas kernels, body(): pl.pallas_call(kernel, out_shape=scratch((SPECIES * ROWS, CELLS), f32), i...  28.9 us
    unnamed x1, local copies, waits for them, and re-layouts  0.91 us

profile of v3, /device:TPU:381, one launch (start us, length us, event | category | flops | bytes accessed | tf_op | source)
XLA Modules:
  0.0 29.8 jit_solution(7760399604559603687)
XLA Ops:
  0.0 28.9 %shard_map.100 = f32[1696,128]{1,0:T(8,128)S(1)} custom-call(s32[1,32]{1,0:T(1,128)} %bitcast.8, f32[16,12]{1,0:T(8,128)} %constant.4.clone.tab_hbm, f32[16,16]{1,0:T(8,128)} %constant.5.clone.steps_hbm, f32[1696,128]{1,0:T(8,128)} %bitcast.6, f32[32,128]{1,0:T(8,128)} %theta_hbm.1, f32[53,325]{1,0:T(8,128)} %bitcast.7, f32[53,325]{1,0:T(8,128)} %stoich_hbm.1, ...), custom_call_target="tpu_custom_call" | custom-call | tf_op jit(solution)/shard_map/pallas_call | solution.py:353
  28.9 0.9 %copy.12 = f32[53,32,128]{2,1,0:T(8,128)} copy(f32[53,32,128]{2,1,0:T(8,128)S(1)} %bitcast.5) | data formatting | bytes 1736704

commit v4 on v3

--- a/solution.py
+++ b/solution.py
@@ -88,7 +88,7 @@
     next_to_first = next_to_first - (1 - (gx + gy + nx + ny - 1) // (nx + ny))
     inner, upper = gx % 4, gy // 16
     row_far = (1 - (inner + 3) // 4) * ((gx + nx - 1) // nx) * (2 - jnp.minimum(upper, 1))
-    column_far = (gy % 16) // 15 * ((2 * ny - 2 - gy) // ny) * (2 - inner // 2)
+    column_far = (gy % 16) // 15 * ((2 * ny - 2 - gy) // ny) * 2
     turn = jnp.maximum(jnp.maximum(row_far, column_far), 3 * next_to_first)
 
     pairs = (
@@ -245,13 +245,13 @@
                 if LAG <= at < len(chunks) + LAG:
                     relax(chunks[at - LAG], j)
 
-    def sections_f8(chunks, start, end):
+    def sections_f8(chunks):
         def some(i, _):
             for u in range(UNROLL):
                 section(chunks, i * UNROLL + u, forward_f8, relax_f8)
             return 0
 
-        lax.fori_loop(start // UNROLL, end // UNROLL, some, 0)
+        lax.fori_loop(0, F8_SECTIONS // UNROLL, some, 0)
 
     def sections_bf(chunks):
         for j in range(F8_SECTIONS, F8_SECTIONS + BF_SECTIONS):
@@ -268,9 +268,8 @@
         start = jnp.concatenate(start, 1) if len(start) > 1 else start[0]
         update(c, MOST - 1, start + source)
 
-    sections_f8(EARLY, 0, 3)
+    sections_f8(EARLY)
     send_at(2)
-    sections_f8(EARLY, 3, F8_SECTIONS)
     sections_bf(EARLY)
     for c in EARLY:
         last_section(c)
@@ -301,7 +300,7 @@
     for c in range(CHUNKS, CHUNKS + 2):
         set_base(c)
 
-    sections_f8(LATE, 0, F8_SECTIONS)
+    sections_f8(LATE)
     sections_bf(LATE)
     for c in LATE:
         last_section(c)

time: 30 us -> 31.1 us (1.037)
  the two profiles are of different devices: /device:TPU:381 before, /device:TPU:125 now
where the time goes in v4:
time: 31.1 us; the launch traced here: 30.9 us
  Pallas kernels  30 us (96%)
  local copies, waits for them, and re-layouts  0.91 us (3%)
    pallas_call x1, Pallas kernels, body(): pl.pallas_call(kernel, out_shape=scratch((SPECIES * ROWS, CELLS), f32), i...  30 us
    unnamed x1, local copies, waits for them, and re-layouts  0.91 us

profile of v4, /device:TPU:125, one launch (start us, length us, event | category | flops | bytes accessed | tf_op | source)
XLA Modules:
  0.0 30.9 jit_solution(2818281058000603560)
XLA Ops:
  0.0 30.0 %shard_map.100 = f32[1696,128]{1,0:T(8,128)S(1)} custom-call(s32[1,32]{1,0:T(1,128)} %bitcast.8, f32[16,12]{1,0:T(8,128)} %constant.4.clone.tab_hbm, f32[16,16]{1,0:T(8,128)} %constant.5.clone.steps_hbm, f32[1696,128]{1,0:T(8,128)} %bitcast.6, f32[32,128]{1,0:T(8,128)} %theta_hbm.1, f32[53,325]{1,0:T(8,128)} %bitcast.7, f32[53,325]{1,0:T(8,128)} %stoich_hbm.1, ...), custom_call_target="tpu_custom_call" | custom-call | tf_op jit(solution)/shard_map/pallas_call | solution.py:352
  30.0 0.9 %copy.12 = f32[53,32,128]{2,1,0:T(8,128)} copy(f32[53,32,128]{2,1,0:T(8,128)S(1)} %bitcast.5) | data formatting | bytes 1736704
